TPU v7x, 512 devices: a whole 4x8x8 slice. The times are simulated.
512 devices in a mesh: mom: 128 (over x, z_hi, y), row: 2 (over core), col: 2 (over z_lo).
Axes of the slice: x: 4, y: 8, z: 8 (z_hi: 4, z_lo: 2; z = z_hi * 2 + z_lo), core: 2. Of those that a mesh axis runs over, the one named last changes fastest.
Arguments:
- left_part: bfloat16 [128, 1536, 1536], P('mom', 'row', 'col'), may hold values from -0.15625 to 0.15625
- vertex: bfloat16 [128, 1536, 1536], P('mom', 'row', 'col'), may hold values from -6 to 6
- bubble: float32 [128, 1536], P('mom'), may hold values from 0.25 to 2
- cross_map: int32 [1536, 128], P(('col', 'mom')), may hold values from 0 to 127, each once within a row
Outputs:
- crossed: bfloat16 [1536, 128, 1536], P(('col', 'mom'), None, 'row')
Inputs may be any that keep to these rules, and one draw needn't show every extreme that they name: Each row cross_map[b, :] is a permutation of the 128 transfer momenta.
All inputs are finite; a program needn't handle non-finite values.
Results may differ from a plain program's by a relative error of at most 0.0055.
Values may be sent and summed in bfloat16 or wider, within the bound.
A program may use at most 64 MiB of HBM per device.

v0:
```python
import jax
import jax.numpy as jnp
from jax import lax
from jax.sharding import PartitionSpec as P


def on_device(left_part, vertex, bubble, cross_map):
    left_full = lax.all_gather(left_part, "col", axis=2, tiled=True)
    weighted = (left_full.astype(jnp.float32) * bubble[:, None, :]).astype(jnp.bfloat16)
    local_q = vertex.shape[0]
    col_count = vertex.shape[2]
    row_count = weighted.shape[1]
    momenta = lax.axis_size("mom")
    per_device = col_count // momenta
    sliced = weighted
    first_term = jnp.einsum(
        "qkb,qak->qba",
        lax.all_gather(vertex, "row", axis=1, tiled=True),
        sliced,
        preferred_element_type=jnp.float32,
    )
    first_round = first_term.astype(jnp.bfloat16)
    flipped = jnp.swapaxes(vertex, 1, 2).astype(jnp.float32)
    sliced = weighted
    second_term = jnp.einsum(
        "qbk,qak->qba",
        lax.all_gather(first_round, "row", axis=2, tiled=True),
        sliced,
        preferred_element_type=jnp.float32,
    )
    summed = (flipped + first_term + second_term).astype(jnp.bfloat16)
    summed = summed.reshape(local_q, momenta, per_device, row_count)
    received = lax.all_to_all(summed, "mom", split_axis=1, concat_axis=0, tiled=True)
    regrouped = received.reshape(-1, per_device, received.shape[-1])
    which = jnp.arange(per_device, dtype=jnp.int32)[:, None]
    return regrouped[cross_map, which]


def solution(mesh):
    in_specs = (
        P("mom", "row", "col"),
        P("mom", "row", "col"),
        P("mom", None),
        P(("col", "mom"), None),
    )
    out_specs = P(("col", "mom"), None, "row")
    return jax.shard_map(
        on_device, mesh=mesh, in_specs=in_specs, out_specs=out_specs, check_vma=False
    )
```

profile of v0, /device:TPU:1, one launch (start us, length us, event | category | flops | bytes accessed | tf_op | source)
XLA Modules:
  0.0 189.4 jit_solution(568758023258396575)
XLA Ops:
  6.5 0.0 copy-start.1
  6.5 0.0 all-gather.5.cloned.1.call-start
  6.5 0.7 all-gather.5.cloned.1.call-update
  7.3 0.0 all-gather.7.cloned.1.call-start
  7.3 0.7 all-gather.7.cloned.1.call-update
  8.0 0.0 all-gather.9.cloned.1.call-start
  8.1 0.0 copy-done.1
  8.1 0.0 copy-start
  8.1 51.0 %all-gather.5.cloned.1.call-done = bf16[1,768,1536]{2,1,0:T(8,128)(2,1)} async-done(((bf16[1,768,768]{2,1,0:T(8,128)(2,1)}), bf16[1,768,1536]{2,1,0:T(8,128)(2,1)}) %all-gather.5.cloned.1.call-update) | async-done | bytes 2359312 | tf_op jit(solution)/shard_map/all_gather | solution.py:8
  59.1 23.1 %all-gather.7.cloned.1.call-done = bf16[1,1536,768]{2,1,0:T(8,128)(2,1)} async-done(((bf16[1,768,768]{2,1,0:T(8,128)(2,1)}), bf16[1,1536,768]{2,1,0:T(8,128)(2,1)}) %all-gather.7.cloned.1.call-update) | async-done | bytes 2359312 | tf_op jit(solution)/shard_map/all_gather | solution.py:18
  82.2 6.2 %bitcast_convert_fusion = (bf16[768,768]{1,0:T(8,128)(2,1)}, f32[768,768]{0,1:T(8,128)}) fusion(bf16[1,1536,768]{2,1,0:T(8,128)(2,1)} %all-gather.7.cloned.1.call-done, bf16[1,768,1536]{2,1,0:T(8,128)(2,1)} %all-gather.5.cloned.1.call-done, f32[1536]{0:T(1024)S(1)} %reduce), kind=kOutput, calls=%fused_computation.6 | convolution fusion | flops 1816068096 | bytes 8263680 | tf_op jit(solution)/shard_map/qkb,qak->qba/dot_general | solution.py:16
  88.4 0.0 all-gather.9.cloned.1.call-update
  88.4 0.0 copy-done
  88.4 0.6 copy.9
  89.1 19.9 %all-gather.9.cloned.1.call-done = bf16[768,1536]{1,0:T(8,128)(2,1)} async-done(((bf16[768,768]{1,0:T(8,128)(2,1)}), bf16[768,1536]{1,0:T(8,128)(2,1)}) %all-gather.9.cloned.1.call-update) | async-done | bytes 2359312 | tf_op jit(solution)/shard_map/all_gather | solution.py:27
  109.0 5.1 %fusion.2 = bf16[1,768,768]{2,1,0:T(8,128)(2,1)S(1)} fusion(f32[768,768]{0,1:T(8,128)} %get-tuple-element.6, bf16[1,768,768]{1,2,0:T(8,128)(2,1)S(1)} %copy.9, bf16[768,1536]{1,0:T(8,128)(2,1)} %all-gather.9.cloned.1.call-done, bf16[1,768,1536]{2,1,0:T(8,128)(2,1)} %all-gather.5.cloned.1.call-done, f32[1536]{0:T(1024)S(1)} %reduce), kind=kOutput, calls=%fused_computation.5 | convolution fusion | flops 1817837568 | bytes 9443328 | tf_op jit(solution)/shard_map/qbk,qak->qba/dot_general | solution.py:25
  114.1 0.0 copy-start.2
  114.1 1.4 reshape.31
  115.5 15.6 %all-to-all-start = ((bf16[1,128,6,768]{3,2,0,1:T(8,128)(2,1)}), bf16[1,128,6,768]{3,2,0,1:T(8,128)(2,1)S(1)}, u32[]{:S(2)}, u32[]{:S(2)}) async-start(bf16[1,128,6,768]{3,2,0,1:T(8,128)(2,1)} %bitcast.6), calls=%async_computation | async-start | bytes 3145728 | tf_op jit(solution)/shard_map/all_to_all | solution.py:33
  131.1 0.0 copy-done.2
  131.2 43.0 %all-to-all-done = bf16[1,128,6,768]{3,2,0,1:T(8,128)(2,1)S(1)} async-done(((bf16[1,128,6,768]{3,2,0,1:T(8,128)(2,1)}), bf16[1,128,6,768]{3,2,0,1:T(8,128)(2,1)S(1)}, u32[]{:S(2)}, u32[]{:S(2)}) %all-to-all-start) | async-done | bytes 1179680 | tf_op jit(solution)/shard_map/all_to_all | solution.py:33
  174.2 0.2 copy.13
  174.4 8.5 %gather_fusion = bf16[768,768]{1,0:T(8,128)(2,1)} fusion(bf16[128,6,768]{2,0,1:T(8,128)(2,1)S(1)} %bitcast.40, s32[768]{0:T(1024)S(1)} %fusion.14), kind=kCustom, calls=%fused_computation | custom fusion | bytes 2365440 | tf_op jit(solution)/shard_map/gather | solution.py:36
  (2 shorter events, 0.0 us)
Async XLA Ops:
  6.5 1.5 copy-start.1
  6.5 52.5 %all-gather.5.cloned.1.call-start = ((), (), s32[]{:S(2)}) async-start(), calls=%async_computation.1 | async-start | bytes 3538944 | tf_op jit(solution)/shard_map/all_gather | solution.py:8
  7.3 74.9 %all-gather.7.cloned.1.call-start = ((), (), s32[]{:S(2)}) async-start(), calls=%async_computation.2 | async-start | bytes 3538944 | tf_op jit(solution)/shard_map/all_gather | solution.py:18
  8.0 101.0 %all-gather.9.cloned.1.call-start = ((), (), s32[]{:S(2)}) async-start(), calls=%async_computation.3 | async-start | bytes 3538944 | tf_op jit(solution)/shard_map/all_gather | solution.py:27
  8.1 80.3 %copy-start = (bf16[1,768,768]{2,1,0:T(8,128)(2,1)S(1)}, bf16[1,768,768]{2,1,0:T(8,128)(2,1)}, u32[]{:S(2)}) copy-start(bf16[1,768,768]{2,1,0:T(8,128)(2,1)} %param.5) | copy-start | bytes 3538948
  114.1 17.0 %copy-start.2 = (s32[6,128]{1,0:T(8,128)S(1)}, s32[6,128]{1,0:T(8,128)}, u32[]{:S(2)}) copy-start(s32[6,128]{1,0:T(8,128)} %param.7) | copy-start | bytes 9220
  115.5 58.7 %all-to-all-start = ((bf16[1,128,6,768]{3,2,0,1:T(8,128)(2,1)}), bf16[1,128,6,768]{3,2,0,1:T(8,128)(2,1)S(1)}, u32[]{:S(2)}, u32[]{:S(2)}) async-start(bf16[1,128,6,768]{3,2,0,1:T(8,128)(2,1)} %bitcast.6), calls=%async_computation | async-start | bytes 3145728 | tf_op jit(solution)/shard_map/all_to_all | solution.py:33
Sparse Core Ops, SparseCore 0:
  9.4 49.5 all-gather.4
  61.2 20.9 all-gather.6
  88.5 20.3 all-gather.8
where the time goes:
time: 190 us; the launch traced here: 189 us
  waiting for transfers between devices  138 us (73%)
  starting transfers between devices  15.7 us (8%)
  between operations  13.2 us (7%)
  matrix products  11.3 us (6%)
  local copies, waits for them, and re-layouts  10.8 us (6%)
    all_gather x1, waiting for transfers between devices, on_device(): left_full = lax.all_gather(left_part, 'col', axis=2, tiled=True)  51 us
    all_to_all x1, waiting for transfers between devices, on_device(): lax.all_to_all(summed, 'mom', split_axis=1, concat_axis=0, tiled=True)  43 us
    all_gather x1, waiting for transfers between devices, on_device(): lax.all_gather(vertex, 'row', axis=1, tiled=True)  23.1 us
    all_gather x1, waiting for transfers between devices, on_device(): lax.all_gather(first_round, 'row', axis=2, tiled=True)  19.9 us
    all_to_all x1, starting transfers between devices, on_device(): lax.all_to_all(summed, 'mom', split_axis=1, concat_axis=0, tiled=True)  15.6 us
    gather x1, local copies, waits for them, and re-layouts, on_device(): return regrouped[cross_map, which]  8.53 us
    dot_general x1, matrix products, on_device(): jnp.einsum('qkb,qak->qba', lax.all_gather(vertex, 'row', axis=1, tiled=Tr...  6.21 us
    dot_general x1, matrix products, on_device(): jnp.einsum('qbk,qak->qba', lax.all_gather(first_round, 'row', axis=2, til...  5.12 us
  transfers between devices with their start and end apart: 4, of which 4 were waited for; matrix products, arithmetic and copies ran while one was open for 0% of the time, Pallas kernels for 0%

commit v1 on v0

v1 whole, which is shorter than its diff:
```python
import functools

import jax
import jax.numpy as jnp
from jax import lax
from jax.experimental import pallas as pl
from jax.experimental.pallas import tpu as pltpu
from jax.sharding import PartitionSpec as P

MESH = pl.DeviceIdType.MESH
F32 = jnp.float32
BF16 = jnp.bfloat16
LANES = 128


def nt(lhs, rhs):
    return lax.dot_general(lhs, rhs, (((1,), (1,)), ((), ())), preferred_element_type=F32)


def kernel(
    momenta, left_ref, vertex_ref, bubble_ref, map_ref, out_ref,
    left_own, left_got, vertex_own, vertex_got, weighted, flipped, first, first_round,
    choose, sent, got, result,
    local_sem, left_send, left_recv, vertex_send, vertex_recv, first_send, first_recv,
    move_send, move_recv, keep_sem, out_sem,
):
    half = left_own.shape[0]
    per_device = half // momenta
    parts, _, span = result.shape
    blocks = span // LANES
    chunks = left_send.shape[0]
    rows = half // chunks
    me = lax.axis_index("mom")
    row = lax.axis_index("row")
    col = lax.axis_index("col")
    across = {"col": 1 - col}
    beside = {"row": 1 - row}

    barrier = pltpu.get_barrier_semaphore()
    pl.semaphore_signal(barrier, inc=1, device_id=across, device_id_type=MESH)
    pl.semaphore_signal(barrier, inc=1, device_id=beside, device_id_type=MESH)

    def greet(step, carry):
        pl.semaphore_signal(barrier, inc=1, device_id={"mom": me ^ step}, device_id_type=MESH)
        return carry

    lax.fori_loop(1, momenta, greet, 0)
    load_vertex = pltpu.make_async_copy(vertex_ref.at[0], vertex_own, local_sem.at[0])
    load_left = pltpu.make_async_copy(left_ref.at[0], left_own, local_sem.at[1])
    load_vertex.start()
    load_left.start()
    pl.semaphore_wait(barrier, momenta + 1)

    left_moves = []
    for n in range(chunks):
        move = pltpu.make_async_remote_copy(
            src_ref=left_ref.at[0, n * rows:(n + 1) * rows],
            dst_ref=left_got.at[n * rows:(n + 1) * rows],
            send_sem=left_send.at[n], recv_sem=left_recv.at[n],
            device_id=across, device_id_type=MESH,
        )
        move.start()
        left_moves.append(move)
    vertex_move = pltpu.make_async_remote_copy(
        src_ref=vertex_ref.at[0], dst_ref=vertex_got,
        send_sem=vertex_send, recv_sem=vertex_recv,
        device_id=beside, device_id_type=MESH,
    )
    vertex_move.start()

    for j in range(per_device):
        wanted = jnp.transpose(jnp.broadcast_to(map_ref[j:j + 1, :], (8, momenta)))[:, 0:1]
        place = lax.broadcasted_iota(jnp.int32, (momenta, half), 1)
        hit = place == wanted * per_device + j
        choose[j * momenta:(j + 1) * momenta, :] = jnp.where(hit, 1.0, 0.0).astype(BF16)

    load_vertex.wait()
    flipped[row] = jnp.transpose(vertex_own[...])
    load_left.wait()
    own_scale = bubble_ref[0:1, pl.ds(pl.multiple_of(col * half, LANES), half)]
    weighted[col] = (left_own[...].astype(F32) * own_scale).astype(BF16)
    vertex_move.wait()
    flipped[1 - row] = jnp.transpose(vertex_got[...])

    first[...] = nt(flipped[col], weighted[col])

    other_scale = bubble_ref[0:1, pl.ds(pl.multiple_of((1 - col) * half, LANES), half)]
    first_moves = []
    for n in range(chunks):
        left_moves[n].wait_recv()
        here = slice(n * rows, (n + 1) * rows)
        weighted[1 - col, here, :] = (left_got[here, :].astype(F32) * other_scale).astype(BF16)
        total = first[:, here] + nt(flipped[1 - col], weighted[1 - col, here, :])
        first[:, here] = total
        first_round[row, :, here] = total.astype(BF16)
        move = pltpu.make_async_remote_copy(
            src_ref=first_round.at[row, :, here], dst_ref=first_round.at[row, :, here],
            send_sem=first_send.at[n], recv_sem=first_recv.at[n],
            device_id=beside, device_id_type=MESH,
        )
        move.start()
        first_moves.append(move)
    for move in first_moves:
        move.wait_recv()

    sent_rows = sent.reshape(sent.shape[0], half, LANES)
    got_rows = got.reshape(got.shape[0], half, LANES)
    for part in range(parts):
        here = slice(part * span, (part + 1) * span)
        total = (
            nt(first_round[0], weighted[0, here, :])
            + nt(first_round[1], weighted[1, here, :])
            + first[:, here]
            + flipped[row, :, here].astype(F32)
        ).astype(BF16)
        for b in range(blocks):
            sent_rows[part * blocks + b] = total[:, b * LANES:(b + 1) * LANES]
        these = slice(part * blocks, (part + 1) * blocks)
        pltpu.make_async_copy(sent.at[these, me], got.at[these, me], keep_sem.at[part]).start()

        def send(step, carry, these=these, part=part):
            to = me ^ step
            pltpu.make_async_remote_copy(
                src_ref=sent.at[these, to], dst_ref=got.at[these, me],
                send_sem=move_send.at[part], recv_sem=move_recv.at[part],
                device_id={"mom": to}, device_id_type=MESH,
            ).start()
            return carry

        lax.fori_loop(1, momenta, send, 0)

    out_moves = []
    for part in range(parts):
        these = slice(part * blocks, (part + 1) * blocks)
        pltpu.make_async_copy(sent.at[these, me], got.at[these, me], keep_sem.at[part]).wait()
        everyone = pl.ds(0, momenta - 1)
        pltpu.make_async_remote_copy(
            src_ref=sent.at[these, everyone], dst_ref=got.at[these, everyone],
            send_sem=move_send.at[part], recv_sem=move_recv.at[part],
            device_id={"mom": me ^ 1}, device_id_type=MESH,
        ).wait()
        values = jnp.concatenate([got_rows[part * blocks + b] for b in range(blocks)], axis=1)
        picked = jnp.dot(choose[...], values, preferred_element_type=F32)
        result[part] = picked.astype(BF16)
        for j in range(per_device):
            move = pltpu.make_async_copy(
                result.at[part, j * momenta:(j + 1) * momenta, :],
                out_ref.at[j, :, part * span:(part + 1) * span],
                out_sem.at[part, j],
            )
            move.start()
            out_moves.append(move)
    for move in left_moves + first_moves:
        move.wait_send()
    for move in out_moves:
        move.wait()


def on_device(left_part, vertex, bubble, cross_map):
    momenta = lax.axis_size("mom")
    half = vertex.shape[2]
    per_device = half // momenta
    chunks = 6 if half % (6 * LANES) == 0 else half // LANES
    parts = 3 if half % (3 * LANES) == 0 else 1
    span = half // parts
    any_space = pl.BlockSpec(memory_space=pl.ANY)
    in_vmem = pl.BlockSpec(memory_space=pltpu.VMEM)
    dma = pltpu.SemaphoreType.DMA
    square = pltpu.VMEM((half, half), BF16)
    pair = pltpu.VMEM((2, half, half), BF16)
    moved = pltpu.VMEM((half // LANES, momenta, per_device // 2, 2, LANES), BF16)
    return pl.pallas_call(
        functools.partial(kernel, momenta),
        out_shape=jax.ShapeDtypeStruct((per_device, momenta, half), BF16),
        in_specs=[any_space, any_space, in_vmem, in_vmem],
        out_specs=any_space,
        scratch_shapes=[
            square, square, square, square, pair, pair,
            pltpu.VMEM((half, half), F32), pair,
            square, moved, moved, pltpu.VMEM((parts, half, span), BF16),
            dma((2,)), dma((chunks,)), dma((chunks,)), dma, dma, dma((chunks,)), dma((chunks,)),
            dma((parts,)), dma((parts,)), dma((parts,)), dma((parts, per_device)),
        ],
        compiler_params=pltpu.CompilerParams(
            collective_id=0, has_side_effects=True, vmem_limit_bytes=56 * 2**20
        ),
        cost_estimate=pl.CostEstimate(
            flops=10 * half**3, bytes_accessed=6 * half * half, transcendentals=0
        ),
    )(left_part, vertex, bubble, cross_map)


def solution(mesh):
    in_specs = (
        P("mom", "row", "col"),
        P("mom", "row", "col"),
        P("mom", None),
        P(("col", "mom"), None),
    )
    out_specs = P(("col", "mom"), None, "row")
    return jax.shard_map(
        on_device, mesh=mesh, in_specs=in_specs, out_specs=out_specs, check_vma=False
    )
```

time: 190 us -> 84 us (0.44)
  waiting for transfers between devices: 138 us -> 0 us
  Pallas kernels: 0 us -> 81.4 us
  starting transfers between devices: 15.7 us -> 0 us
  between operations: 13.2 us -> 0.01 us
  matrix products: 11.3 us -> 0 us
  local copies, waits for them, and re-layouts: 10.8 us -> 2.36 us
    all_gather x3 -> x0, waiting for transfers between devices: 94 us -> none  [the longest x1 51 us: on_device(): left_full = lax.all_gather(left_part, 'col', axis=2, tiled=True)]
    pallas_call x0 -> x1, Pallas kernels: none -> 81.4 us  [on_device(): pl.pallas_call(functools.partial(kernel, momenta), out_shape=jax.ShapeDty...]
    all_to_all x1 -> x0, waiting for transfers between devices: 43 us -> none  [on_device(): lax.all_to_all(summed, 'mom', split_axis=1, concat_axis=0, tiled=True)]
    all_to_all x1 -> x0, starting transfers between devices: 15.6 us -> none  [on_device(): lax.all_to_all(summed, 'mom', split_axis=1, concat_axis=0, tiled=True)]
    dot_general x2 -> x0, matrix products: 11.3 us -> none  [the longest x1 6.21 us: on_device(): jnp.einsum('qkb,qak->qba', lax.all_gather(vertex, 'row', axis=1, tiled=Tr...]
    gather x1 -> x0, local copies, waits for them, and re-layouts: 8.53 us -> none  [on_device(): return regrouped[cross_map, which]]
  transfers between devices with their start and end apart: 4 -> 0, of which waited for: 4 -> 0; matrix products, arithmetic and copies ran while one was open for 0% -> 0% of each run, Pallas kernels for 0% -> 0%
where the time goes in v1:
time: 84 us; the launch traced here: 83.8 us
  Pallas kernels  81.4 us (97%)
  local copies, waits for them, and re-layouts  2.36 us (3%)
    pallas_call x1, Pallas kernels, on_device(): pl.pallas_call(functools.partial(kernel, momenta), out_shape=jax.ShapeDty...  81.4 us
    unnamed x1, local copies, waits for them, and re-layouts  2.36 us

profile of v1, /device:TPU:1, one launch (start us, length us, event | category | flops | bytes accessed | tf_op | source)
XLA Modules:
  0.0 83.8 jit_solution(1087563971881733614)
XLA Ops:
  0.0 81.4 %shard_map.46 = bf16[6,128,768]{2,1,0:T(8,128)(2,1)} custom-call(bf16[1,768,768]{2,1,0:T(8,128)(2,1)} %left_ref.1, bf16[1,768,768]{2,1,0:T(8,128)(2,1)} %vertex_ref.1, f32[1,1536]{1,0:T(1,128)} %bubble_ref.1, s32[6,128]{1,0:T(8,128)} %map_ref.1), custom_call_target="tpu_custom_call" | custom-call | flops 4529848320 | bytes 3538944 | tf_op jit(solution)/shard_map/pallas_call | solution.py:172
  81.4 2.4 %copy.6 = bf16[6,128,768]{2,1,0:T(8,128)(2,1)} copy(bf16[6,128,768]{2,1,0:T(8,128)(2,1)} %shard_map.46) | data formatting | bytes 2359296

commit v2 on v1

--- a/solution.py
+++ b/solution.py
@@ -11,6 +11,7 @@
 F32 = jnp.float32
 BF16 = jnp.bfloat16
 LANES = 128
+UNROLL = 4
 
 
 def nt(lhs, rhs):
@@ -20,16 +21,16 @@
 def kernel(
     momenta, left_ref, vertex_ref, bubble_ref, map_ref, out_ref,
     left_own, left_got, vertex_own, vertex_got, weighted, flipped, first, first_round,
-    choose, sent, got, result,
+    choose, sent, got,
     local_sem, left_send, left_recv, vertex_send, vertex_recv, first_send, first_recv,
-    move_send, move_recv, keep_sem, out_sem,
+    move_send, move_recv, keep_sem, round_sem,
 ):
     half = left_own.shape[0]
     per_device = half // momenta
-    parts, _, span = result.shape
+    parts = move_send.shape[0]
+    span = half // parts
     blocks = span // LANES
-    chunks = left_send.shape[0]
-    rows = half // chunks
+    pieces, chunks = left_send.shape[0], first_send.shape[0]
     me = lax.axis_index("mom")
     row = lax.axis_index("row")
     col = lax.axis_index("col")
@@ -37,22 +38,20 @@
     beside = {"row": 1 - row}
 
     barrier = pltpu.get_barrier_semaphore()
+    rounds = round_sem.shape[0]
     pl.semaphore_signal(barrier, inc=1, device_id=across, device_id_type=MESH)
     pl.semaphore_signal(barrier, inc=1, device_id=beside, device_id_type=MESH)
-
-    def greet(step, carry):
-        pl.semaphore_signal(barrier, inc=1, device_id={"mom": me ^ step}, device_id_type=MESH)
-        return carry
-
-    lax.fori_loop(1, momenta, greet, 0)
+    for r in range(rounds):
+        pl.semaphore_signal(barrier, inc=1, device_id={"mom": me ^ (1 << r)}, device_id_type=MESH)
     load_vertex = pltpu.make_async_copy(vertex_ref.at[0], vertex_own, local_sem.at[0])
     load_left = pltpu.make_async_copy(left_ref.at[0], left_own, local_sem.at[1])
     load_vertex.start()
     load_left.start()
-    pl.semaphore_wait(barrier, momenta + 1)
+    pl.semaphore_wait(barrier, rounds + 2)
 
     left_moves = []
-    for n in range(chunks):
+    for n in range(pieces):
+        rows = half // pieces
         move = pltpu.make_async_remote_copy(
             src_ref=left_ref.at[0, n * rows:(n + 1) * rows],
             dst_ref=left_got.at[n * rows:(n + 1) * rows],
@@ -68,26 +67,47 @@
     )
     vertex_move.start()
 
+    def call(r):
+        if r < rounds:
+            pl.semaphore_signal(
+                round_sem.at[r], inc=1, device_id={"mom": me ^ (1 << r)}, device_id_type=MESH
+            )
+
+    def hear(r):
+        if r < rounds:
+            pl.semaphore_wait(round_sem.at[r], 1)
+            call(r + 1)
+
+    call(0)
+    load_vertex.wait()
+    flipped[row] = jnp.transpose(vertex_own[...])
+    hear(0)
+    load_left.wait()
+    own_scale = bubble_ref[0:1, pl.ds(pl.multiple_of(col * half, LANES), half)]
+    weighted[col] = (left_own[...].astype(F32) * own_scale).astype(BF16)
+    hear(1)
+    vertex_move.wait()
+    flipped[1 - row] = jnp.transpose(vertex_got[...])
+    hear(2)
+    first[...] = nt(flipped[col], weighted[col])
+    hear(3)
     for j in range(per_device):
         wanted = jnp.transpose(jnp.broadcast_to(map_ref[j:j + 1, :], (8, momenta)))[:, 0:1]
         place = lax.broadcasted_iota(jnp.int32, (momenta, half), 1)
         hit = place == wanted * per_device + j
         choose[j * momenta:(j + 1) * momenta, :] = jnp.where(hit, 1.0, 0.0).astype(BF16)
-
-    load_vertex.wait()
-    flipped[row] = jnp.transpose(vertex_own[...])
-    load_left.wait()
-    own_scale = bubble_ref[0:1, pl.ds(pl.multiple_of(col * half, LANES), half)]
-    weighted[col] = (left_own[...].astype(F32) * own_scale).astype(BF16)
-    vertex_move.wait()
-    flipped[1 - row] = jnp.transpose(vertex_got[...])
-
-    first[...] = nt(flipped[col], weighted[col])
+        if j % 2 == 1 or j == per_device - 1:
+            hear(4 + j // 2)
+    for r in range(4 + (per_device + 1) // 2, rounds):
+        hear(r)
 
     other_scale = bubble_ref[0:1, pl.ds(pl.multiple_of((1 - col) * half, LANES), half)]
     first_moves = []
+    rows = half // chunks
+    each = pieces // chunks
     for n in range(chunks):
-        left_moves[n].wait_recv()
+        for move in left_moves[n * each:(n + 1) * each]:
+            move.wait_recv()
         here = slice(n * rows, (n + 1) * rows)
         weighted[1 - col, here, :] = (left_got[here, :].astype(F32) * other_scale).astype(BF16)
         total = first[:, here] + nt(flipped[1 - col], weighted[1 - col, here, :])
@@ -100,6 +120,13 @@
         )
         move.start()
         first_moves.append(move)
+    for part in range(parts):
+        here = slice(part * span, (part + 1) * span)
+        first[:, here] = (
+            first[:, here]
+            + flipped[row, :, here].astype(F32)
+            + nt(first_round[row], weighted[row, here, :])
+        )
     for move in first_moves:
         move.wait_recv()
 
@@ -108,10 +135,7 @@
     for part in range(parts):
         here = slice(part * span, (part + 1) * span)
         total = (
-            nt(first_round[0], weighted[0, here, :])
-            + nt(first_round[1], weighted[1, here, :])
-            + first[:, here]
-            + flipped[row, :, here].astype(F32)
+            first[:, here] + nt(first_round[1 - row], weighted[1 - row, here, :])
         ).astype(BF16)
         for b in range(blocks):
             sent_rows[part * blocks + b] = total[:, b * LANES:(b + 1) * LANES]
@@ -127,9 +151,8 @@
             ).start()
             return carry
 
-        lax.fori_loop(1, momenta, send, 0)
-
-    out_moves = []
+        lax.fori_loop(1, momenta, send, 0, unroll=UNROLL)
+
     for part in range(parts):
         these = slice(part * blocks, (part + 1) * blocks)
         pltpu.make_async_copy(sent.at[these, me], got.at[these, me], keep_sem.at[part]).wait()
@@ -141,26 +164,20 @@
         ).wait()
         values = jnp.concatenate([got_rows[part * blocks + b] for b in range(blocks)], axis=1)
         picked = jnp.dot(choose[...], values, preferred_element_type=F32)
-        result[part] = picked.astype(BF16)
         for j in range(per_device):
-            move = pltpu.make_async_copy(
-                result.at[part, j * momenta:(j + 1) * momenta, :],
-                out_ref.at[j, :, part * span:(part + 1) * span],
-                out_sem.at[part, j],
+            out_ref[j, :, part * span:(part + 1) * span] = (
+                picked[j * momenta:(j + 1) * momenta].astype(BF16)
             )
-            move.start()
-            out_moves.append(move)
     for move in left_moves + first_moves:
         move.wait_send()
-    for move in out_moves:
-        move.wait()
 
 
 def on_device(left_part, vertex, bubble, cross_map):
     momenta = lax.axis_size("mom")
     half = vertex.shape[2]
     per_device = half // momenta
-    chunks = 6 if half % (6 * LANES) == 0 else half // LANES
+    chunks = half // LANES
+    pieces = 2 * chunks
     parts = 3 if half % (3 * LANES) == 0 else 1
     span = half // parts
     any_space = pl.BlockSpec(memory_space=pl.ANY)
@@ -171,15 +188,16 @@
     moved = pltpu.VMEM((half // LANES, momenta, per_device // 2, 2, LANES), BF16)
     return pl.pallas_call(
         functools.partial(kernel, momenta),
-        out_shape=jax.ShapeDtypeStruct((per_device, momenta, half), BF16),
+        out_shape=pltpu.VMEM((per_device, momenta, half), BF16),
         in_specs=[any_space, any_space, in_vmem, in_vmem],
-        out_specs=any_space,
+        out_specs=in_vmem,
         scratch_shapes=[
             square, square, square, square, pair, pair,
             pltpu.VMEM((half, half), F32), pair,
-            square, moved, moved, pltpu.VMEM((parts, half, span), BF16),
-            dma((2,)), dma((chunks,)), dma((chunks,)), dma, dma, dma((chunks,)), dma((chunks,)),
-            dma((parts,)), dma((parts,)), dma((parts,)), dma((parts, per_device)),
+            square, moved, moved,
+            dma((2,)), dma((pieces,)), dma((pieces,)), dma, dma, dma((chunks,)), dma((chunks,)),
+            dma((parts,)), dma((parts,)), dma((parts,)),
+            pltpu.SemaphoreType.REGULAR((momenta.bit_length() - 1,)),
         ],
         compiler_params=pltpu.CompilerParams(
             collective_id=0, has_side_effects=True, vmem_limit_bytes=56 * 2**20

time: 84 us -> 78.4 us (0.933)
  Pallas kernels: 81.4 us -> 77.2 us
  local copies, waits for them, and re-layouts: 2.36 us -> 1.02 us
    pallas_call x1, Pallas kernels: 81.4 us -> 77.2 us  [on_device(): pl.pallas_call(functools.partial(kernel, momenta), out_shape=pltpu.VMEM((...]
    unnamed x1, local copies, waits for them, and re-layouts: 2.36 us -> 1.02 us
where the time goes in v2:
time: 78.4 us; the launch traced here: 78.2 us
  Pallas kernels  77.2 us (98%)
  local copies, waits for them, and re-layouts  1.02 us (1%)
    pallas_call x1, Pallas kernels, on_device(): pl.pallas_call(functools.partial(kernel, momenta), out_shape=pltpu.VMEM((...  77.2 us

profile of v2, /device:TPU:1, one launch (start us, length us, event | category | flops | bytes accessed | tf_op | source)
XLA Modules:
  0.0 78.2 jit_solution(9691627873777124936)
XLA Ops:
  0.0 77.2 %shard_map.46 = bf16[6,128,768]{2,1,0:T(8,128)(2,1)S(1)} custom-call(bf16[1,768,768]{2,1,0:T(8,128)(2,1)} %left_ref.1, bf16[1,768,768]{2,1,0:T(8,128)(2,1)} %vertex_ref.1, f32[1,1536]{1,0:T(1,128)} %bubble_ref.1, s32[6,128]{1,0:T(8,128)} %map_ref.1), custom_call_target="tpu_custom_call" | custom-call | flops 4529848320 | bytes 3538944 | tf_op jit(solution)/shard_map/pallas_call | solution.py:189
  77.2 1.0 %copy.6 = bf16[6,128,768]{2,1,0:T(8,128)(2,1)} copy(bf16[6,128,768]{2,1,0:T(8,128)(2,1)S(1)} %shard_map.46) | data formatting | bytes 2359296

commit v3 on v2

--- a/solution.py
+++ b/solution.py
@@ -178,7 +178,7 @@
     per_device = half // momenta
     chunks = half // LANES
     pieces = 2 * chunks
-    parts = 3 if half % (3 * LANES) == 0 else 1
+    parts = 6 if half % (6 * LANES) == 0 else 1
     span = half // parts
     any_space = pl.BlockSpec(memory_space=pl.ANY)
     in_vmem = pl.BlockSpec(memory_space=pltpu.VMEM)

time: 78.4 us -> 78.1 us (level)
  no operation moved by 1% of the time
where the time goes in v3:
time: 78.1 us; the launch traced here: 77.7 us
  Pallas kernels  76.7 us (98%)
  local copies, waits for them, and re-layouts  1.02 us (1%)
    pallas_call x1, Pallas kernels, on_device(): pl.pallas_call(functools.partial(kernel, momenta), out_shape=pltpu.VMEM((...  76.7 us

profile of v3, /device:TPU:1, one launch (start us, length us, event | category | flops | bytes accessed | tf_op | source)
XLA Modules:
  0.0 77.7 jit_solution(11144517601856710193)
XLA Ops:
  0.0 76.7 %shard_map.46 = bf16[6,128,768]{2,1,0:T(8,128)(2,1)S(1)} custom-call(bf16[1,768,768]{2,1,0:T(8,128)(2,1)} %left_ref.1, bf16[1,768,768]{2,1,0:T(8,128)(2,1)} %vertex_ref.1, f32[1,1536]{1,0:T(1,128)} %bubble_ref.1, s32[6,128]{1,0:T(8,128)} %map_ref.1), custom_call_target="tpu_custom_call" | custom-call | flops 4529848320 | bytes 3538944 | tf_op jit(solution)/shard_map/pallas_call | solution.py:189
  76.7 1.0 %copy.6 = bf16[6,128,768]{2,1,0:T(8,128)(2,1)} copy(bf16[6,128,768]{2,1,0:T(8,128)(2,1)S(1)} %shard_map.46) | data formatting | bytes 2359296
